TPU v7x, 512 devices: a whole 4x4x16 slice. The times are simulated.
512 devices in a mesh: row: 32 (over y, z_hi, core), col: 16 (over z_lo, x).
Axes of the slice: x: 4, y: 4, z: 16 (z_hi: 4, z_lo: 4; z = z_hi * 4 + z_lo), core: 2. Of those that a mesh axis runs over, the one named last changes fastest.
Arguments:
- alignment: float32 [768, 64, 64], P('row', 'col'), may hold values from -6 to 6
- pair_state: float32 [768, 768, 128], P('row', 'col'), may hold values from -6 to 6
- pair_weights: float32 [8, 768, 768], P(None, 'row', 'col'), may hold values from 0 to 1, as said below
- align_gain: float32 [64], replicated, may hold values from 0.5 to 2
- value_weight: float32 [64, 256], replicated, may hold values from -0.75 to 0.75
- gate_weight: float32 [64, 256], replicated, may hold values from -0.75 to 0.75
- output_weight: float32 [256, 64], replicated, may hold values from -0.375 to 0.375
- outer_gain: float32 [64], replicated, may hold values from 0.5 to 2
- left_weight: float32 [64, 32], replicated, may hold values from -0.75 to 0.75
- right_weight: float32 [64, 32], replicated, may hold values from -0.75 to 0.75
- outer_weight: float32 [1024, 128], replicated, may hold values from -0.75 to 0.75
- outer_bias: float32 [128], replicated, may hold values from -3 to 3
Outputs:
- alignment_out: float32 [768, 64, 64], P('row', 'col')
- pair_out: float32 [768, 768, 128], P('row', 'col')
Inputs may be any that keep to these rules, and one draw needn't show every extreme that they name: `pair_weights`: every entry is positive, and for each head and row token the weights over the 768 column tokens sum to one.
All inputs are finite; a program needn't handle non-finite values.
Results may differ from a plain program's by a relative error of at most 0.00011.
Values sent between devices are 32-bit elements; how exact they have to be, the bound alone decides.
No kernel may reach another device: no remote copies, remote signals or barrier semaphores. Data moves between devices by JAX's collectives and lax.ppermute only.
A program may use at most 64 MiB of HBM per device.

v0:
```python
import jax
import jax.numpy as jnp
from jax import lax
from jax.sharding import PartitionSpec as P

PRECISE = lax.Precision.HIGHEST


def from_everyone(value, axis):
    count = lax.axis_size(axis)
    return lax.all_to_all(
        jnp.broadcast_to(value[None], (count, *value.shape)), axis, 0, 0, tiled=True
    )


def in_order(tiles, dim):
    tiles = jnp.moveaxis(tiles, 0, dim)
    lengths = tiles.shape
    return tiles.reshape(*lengths[:dim], lengths[dim] * lengths[dim + 1], *lengths[dim + 2 :])


def collect(value, axis, dim):
    tiles = from_everyone(value, axis)
    return in_order(tiles, dim)


def normalize(features, channel_gain):
    channel_mean = jnp.mean(features, axis=-1, keepdims=True)
    centered = features - channel_mean
    spread = jnp.mean(centered * centered, axis=-1, keepdims=True)
    return centered * lax.rsqrt(spread + 1e-05) * channel_gain


def on_device(
    alignment,
    pair_state,
    pair_weights,
    align_gain,
    value_weight,
    gate_weight,
    output_weight,
    outer_gain,
    left_weight,
    right_weight,
    outer_weight,
    outer_bias,
):
    head_count = pair_weights.shape[0]
    local_rows = alignment.shape[0]
    local_seqs = alignment.shape[1]
    channels = alignment.shape[2]
    normed = normalize(alignment, align_gain)
    flat_normed = normed.reshape(local_rows, local_seqs * channels)
    gathered = lax.all_gather(flat_normed, "row", axis=0, tiled=True)
    gathered = gathered.reshape(-1, local_seqs, channels)
    mixed_rows = jnp.einsum(
        "hij,jsc->ishc", collect(pair_weights, "col", 2), gathered, precision=PRECISE
    )
    per_head = value_weight.reshape(channels, head_count, -1)
    averaged = jnp.einsum("ishc,chd->ishd", mixed_rows, per_head, precision=PRECISE)
    gate_values = jax.nn.sigmoid(jnp.einsum("nsc,cd->nsd", normed, gate_weight, precision=PRECISE))
    gated_heads = gate_values * averaged.reshape(gate_values.shape)
    alignment_out = alignment + jnp.einsum(
        "nsd,dc->nsc", gated_heads, output_weight, precision=PRECISE
    )
    normed_out = normalize(alignment_out, outer_gain)
    left_side = jnp.einsum("nsc,cd->nsd", normed_out, left_weight, precision=PRECISE)
    right_side = jnp.einsum("nsc,cd->nsd", normed_out, right_weight, precision=PRECISE)
    factor_width = left_side.shape[2]
    columns = pair_state.shape[1]
    left_flat = left_side.transpose(1, 0, 2).reshape(local_seqs, local_rows * factor_width)
    right_rows = right_side.reshape(local_rows, local_seqs * factor_width)
    right_tokens = collect(right_rows, "row", 0)
    right_tokens = right_tokens.reshape(-1, local_seqs, factor_width)
    right_columns = lax.all_to_all(right_tokens, "col", split_axis=0, concat_axis=1, tiled=True)
    right_all = right_columns.transpose(1, 0, 2)
    left_all = collect(left_flat, "col", 0)
    sequences = left_all.shape[0]
    left_all = left_all.reshape(sequences, local_rows, factor_width)
    block_rows = 8
    left_blocks = left_all.reshape(
        sequences, local_rows // block_rows, block_rows, factor_width
    ).transpose(1, 2, 0, 3)

    def outer_block(left_block):
        product = jnp.einsum("isc,sjd->ijcd", left_block, right_all, precision=PRECISE) / sequences
        flattened = product.reshape(-1, factor_width * factor_width)
        projected = jnp.dot(
            flattened, outer_weight, precision=PRECISE, preferred_element_type=jnp.float32
        )
        return projected.reshape(block_rows, columns, -1)

    update = lax.map(outer_block, left_blocks).reshape(pair_state.shape)
    pair_out = pair_state + update + outer_bias
    return (alignment_out, pair_out)


def solution(mesh):
    return jax.shard_map(
        on_device,
        mesh=mesh,
        in_specs=(
            P("row", "col", None),
            P("row", "col", None),
            P(None, "row", "col"),
            P(),
            P(),
            P(),
            P(),
            P(),
            P(),
            P(),
            P(),
            P(),
        ),
        out_specs=(P("row", "col", None), P("row", "col", None)),
        check_vma=False,
    )
```

profile of v0, /device:TPU:8, one launch (start us, length us, event | category | flops | bytes accessed | tf_op | source)
XLA Modules:
  0.0 219.8 jit_solution(15116444611378009533)
XLA Ops:
  0.6 1.1 broadcast_in_dim.13
  1.7 2.4 %reshape.79 = f32[16,1,9216]{2,1,0:T(1,128)} reshape(f32[16,8,24,48]{3,2,1,0:T(8,128)S(1)} %broadcast_in_dim.13) | data formatting | bytes 1179648
  4.1 8.5 %all-to-all-start = ((f32[16,1,9216]{2,1,0:T(1,128)}), f32[16,1,9216]{2,1,0:T(1,128)S(1)}, u32[]{:S(2)}, u32[]{:S(2)}) async-start(f32[16,1,9216]{2,1,0:T(1,128)} %reshape.79), calls=%async_computation | async-start | bytes 1179648 | tf_op jit(solution)/shard_map/all_to_all | solution.py:11
  13.2 58.9 %all_gather.3 = f32[768,256]{1,0:T(8,128)S(1)} all-gather(f32[24,256]{1,0:T(8,128)S(1)} %reshape.62), channel_id=1, replica_groups=mesh['row'=32,'col'=16] {'row'}, dimensions={0}, use_global_device_ids=true | all-gather | bytes 811008 | tf_op jit(solution)/shard_map/all_gather | solution.py:54
  72.0 1.2 copy.71
  73.8 2.0 reduce
  76.5 0.9 copy.72
  78.6 1.1 convolution_bitcast_fusion.2
  81.8 0.8 broadcast_in_dim.19
  82.6 10.2 %all-to-all-start.2 = ((f32[32,24,128]{2,1,0:T(8,128)}), f32[32,24,128]{2,1,0:T(8,128)S(1)}, u32[]{:S(2)}, u32[]{:S(2)}) async-start(f32[32,24,128]{2,1,0:T(8,128)} %broadcast_in_dim.19), calls=%async_computation.2 | async-start | bytes 786432 | tf_op jit(solution)/shard_map/all_to_all | solution.py:11
  93.1 19.2 %all-to-all-done.2 = f32[32,24,128]{2,1,0:T(8,128)S(1)} async-done(((f32[32,24,128]{2,1,0:T(8,128)}), f32[32,24,128]{2,1,0:T(8,128)S(1)}, u32[]{:S(2)}, u32[]{:S(2)}) %all-to-all-start.2) | async-done | bytes 393248 | tf_op jit(solution)/shard_map/all_to_all | solution.py:11
  113.0 13.8 %all-to-all-start.1 = ((f32[16,4,768]{2,1,0:T(4,128)}), f32[16,4,768]{2,1,0:T(4,128)S(1)}, u32[]{:S(2)}, u32[]{:S(2)}) async-start(f32[16,4,768]{2,1,0:T(4,128)} %broadcast_in_dim.16), calls=%async_computation.1 | async-start | bytes 393216 | tf_op jit(solution)/shard_map/all_to_all | solution.py:11
  127.5 1.8 reshape.81
  129.3 8.0 %all-to-all-done.1 = f32[16,4,768]{2,1,0:T(4,128)S(1)} async-done(((f32[16,4,768]{2,1,0:T(4,128)}), f32[16,4,768]{2,1,0:T(4,128)S(1)}, u32[]{:S(2)}, u32[]{:S(2)}) %all-to-all-start.1) | async-done | bytes 196640 | tf_op jit(solution)/shard_map/all_to_all | solution.py:11
  137.2 3.7 %all-to-all-start.3 = ((f32[16,1,6144]{2,1,0:T(1,128)}), f32[16,1,6144]{2,1,0:T(1,128)S(1)}, u32[]{:S(2)}, u32[]{:S(2)}) async-start(f32[16,1,6144]{2,1,0:T(1,128)} %reshape.81), calls=%async_computation.3 | async-start | bytes 786432 | tf_op jit(solution)/shard_map/all_to_all | solution.py:75
  142.2 11.7 %all-to-all-done.3 = f32[16,1,6144]{2,1,0:T(1,128)S(1)} async-done(((f32[16,1,6144]{2,1,0:T(1,128)}), f32[16,1,6144]{2,1,0:T(1,128)S(1)}, u32[]{:S(2)}, u32[]{:S(2)}) %all-to-all-start.3) | async-done | bytes 393248 | tf_op jit(solution)/shard_map/all_to_all | solution.py:75
  153.8 1.6 reduce.1
  155.4 0.8 reshape.82
  157.9 59.8 %while.10 = (s32[]{:T(128)}, f32[3,8,48,128]{3,2,1,0:T(8,128)}, f32[3,8,64,32]{2,3,1,0:T(8,128)S(1)}, f32[64,48,32]{0,1,2:T(8,128)S(1)}, f32[1024,128]{1,0:T(8,128)S(1)}, /*index=5*/s32[]{:T(128)}) while((s32[]{:T(128)}, f32[3,8,48,128]{3,2,1,0:T(8,128)}, f32[3,8,64,32]{2,3,1,0:T(8,128)S(1)}, f32[64,48,32]{0,1,2:T(8,128)S(1)}, ...), condition=%wide.region_5.6_spmd, body=%wide.region_4.5_spmd.sunk | while | flops 906362880 | bytes 11076169 | solution.py:93
  157.9 4.9 %multiply_bitcast_fusion.2 = f32[8,48,32,32]{1,2,3,0:T(8,128)} fusion(f32[64,48,32]{0,1,2:T(8,128)S(1)} %get-tuple-element.118, f32[3,8,64,32]{2,3,1,0:T(8,128)S(1)} %get-tuple-element.117, s32[]{:T(128)} %get-tuple-element.109), kind=kOutput, calls=%fused_computation.clone.1 | convolution fusion | flops 302383104 | bytes 2490372 | tf_op jit(solution)/shard_map/while/body/eval_jaxpr/isc,sjd->ijcd/dot_general | solution.py:86
  162.9 7.9 %copy.93 = f32[8,48,32,32]{3,2,1,0:T(8,128)} copy(f32[8,48,32,32]{1,2,3,0:T(8,128)} %multiply_bitcast_fusion.2) | data formatting | bytes 3145728 | tf_op jit(solution)/shard_map/while/body/eval_jaxpr/div | solution.py:86
  170.7 5.0 %reshape.84 = f32[8,48,1024]{2,1,0:T(8,128)S(1)} reshape(f32[8,48,32,32]{3,2,1,0:T(8,128)} %copy.93) | data formatting | bytes 3145728 | tf_op jit(solution)/shard_map/reshape.25
  175.8 2.1 fusion.39
  177.8 4.9 %multiply_bitcast_fusion.2 = f32[8,48,32,32]{1,2,3,0:T(8,128)} fusion(f32[64,48,32]{0,1,2:T(8,128)S(1)} %get-tuple-element.118, f32[3,8,64,32]{2,3,1,0:T(8,128)S(1)} %get-tuple-element.117, s32[]{:T(128)} %get-tuple-element.109), kind=kOutput, calls=%fused_computation.clone.1 | convolution fusion | flops 302383104 | bytes 2490372 | tf_op jit(solution)/shard_map/while/body/eval_jaxpr/isc,sjd->ijcd/dot_general | solution.py:86
  182.8 7.9 %copy.93 = f32[8,48,32,32]{3,2,1,0:T(8,128)} copy(f32[8,48,32,32]{1,2,3,0:T(8,128)} %multiply_bitcast_fusion.2) | data formatting | bytes 3145728 | tf_op jit(solution)/shard_map/while/body/eval_jaxpr/div | solution.py:86
  190.6 5.0 %reshape.84 = f32[8,48,1024]{2,1,0:T(8,128)S(1)} reshape(f32[8,48,32,32]{3,2,1,0:T(8,128)} %copy.93) | data formatting | bytes 3145728 | tf_op jit(solution)/shard_map/reshape.25
  195.7 2.1 fusion.39
  197.8 4.9 %multiply_bitcast_fusion.2 = f32[8,48,32,32]{1,2,3,0:T(8,128)} fusion(f32[64,48,32]{0,1,2:T(8,128)S(1)} %get-tuple-element.118, f32[3,8,64,32]{2,3,1,0:T(8,128)S(1)} %get-tuple-element.117, s32[]{:T(128)} %get-tuple-element.109), kind=kOutput, calls=%fused_computation.clone.1 | convolution fusion | flops 302383104 | bytes 2490372 | tf_op jit(solution)/shard_map/while/body/eval_jaxpr/isc,sjd->ijcd/dot_general | solution.py:86
  202.7 7.9 %copy.93 = f32[8,48,32,32]{3,2,1,0:T(8,128)} copy(f32[8,48,32,32]{1,2,3,0:T(8,128)} %multiply_bitcast_fusion.2) | data formatting | bytes 3145728 | tf_op jit(solution)/shard_map/while/body/eval_jaxpr/div | solution.py:86
  210.6 5.0 %reshape.84 = f32[8,48,1024]{2,1,0:T(8,128)S(1)} reshape(f32[8,48,32,32]{3,2,1,0:T(8,128)} %copy.93) | data formatting | bytes 3145728 | tf_op jit(solution)/shard_map/reshape.25
  215.6 2.1 fusion.39
  217.7 2.1 fusion.10
  (54 shorter events, 9.5 us)
Async XLA Ops:
  0.6 80.0 %copy-start = (f32[64,256]{1,0:T(8,128)S(1)}, f32[64,256]{1,0:T(8,128)}, u32[]{:S(2)}) copy-start(f32[64,256]{1,0:T(8,128)} %param.19) | copy-start | bytes 196612
  1.7 10.9 %copy-start.3 = (f32[24,4,64]{2,1,0:T(4,128)S(1)}, f32[24,4,64]{2,1,0:T(4,128)}, u32[]{:S(2)}) copy-start(f32[24,4,64]{2,1,0:T(4,128)} %param.14) | copy-start | bytes 73732
  1.7 11.2 %copy-start.6 = (f32[64]{0:T(128)S(1)}, f32[64]{0:T(128)}, u32[]{:S(2)}) copy-start(f32[64]{0:T(128)} %param.17) | copy-start | bytes 772
  4.1 69.2 %all-to-all-start = ((f32[16,1,9216]{2,1,0:T(1,128)}), f32[16,1,9216]{2,1,0:T(1,128)S(1)}, u32[]{:S(2)}, u32[]{:S(2)}) async-start(f32[16,1,9216]{2,1,0:T(1,128)} %reshape.79), calls=%async_computation | async-start | bytes 1179648 | tf_op jit(solution)/shard_map/all_to_all | solution.py:11
  12.6 60.6 %copy-start.4 = (f32[64,256]{1,0:T(8,128)S(1)}, f32[64,256]{1,0:T(8,128)}, u32[]{:S(2)}) copy-start(f32[64,256]{1,0:T(8,128)} %param.18) | copy-start | bytes 196612
  77.5 1.1 copy-start.2
  79.7 1.2 copy-start.5
  79.7 1.7 copy-start.8
  79.7 1.7 copy-start.10
  80.2 12.5 %copy-start.9 = (f32[64,32]{0,1:T(8,128)S(1)}, f32[64,32]{0,1:T(8,128)}, u32[]{:S(2)}) copy-start(f32[64,32]{0,1:T(8,128)} %param.22) | copy-start | bytes 24580
  82.6 29.7 %all-to-all-start.2 = ((f32[32,24,128]{2,1,0:T(8,128)}), f32[32,24,128]{2,1,0:T(8,128)S(1)}, u32[]{:S(2)}, u32[]{:S(2)}) async-start(f32[32,24,128]{2,1,0:T(8,128)} %broadcast_in_dim.19), calls=%async_computation.2 | async-start | bytes 786432 | tf_op jit(solution)/shard_map/all_to_all | solution.py:11
  113.0 24.2 %all-to-all-start.1 = ((f32[16,4,768]{2,1,0:T(4,128)}), f32[16,4,768]{2,1,0:T(4,128)S(1)}, u32[]{:S(2)}, u32[]{:S(2)}) async-start(f32[16,4,768]{2,1,0:T(4,128)} %broadcast_in_dim.16), calls=%async_computation.1 | async-start | bytes 393216 | tf_op jit(solution)/shard_map/all_to_all | solution.py:11
  137.2 16.6 %all-to-all-start.3 = ((f32[16,1,6144]{2,1,0:T(1,128)}), f32[16,1,6144]{2,1,0:T(1,128)S(1)}, u32[]{:S(2)}, u32[]{:S(2)}) async-start(f32[16,1,6144]{2,1,0:T(1,128)} %reshape.81), calls=%async_computation.3 | async-start | bytes 786432 | tf_op jit(solution)/shard_map/all_to_all | solution.py:75
  156.9 1.0 copy-start.1
  157.9 59.8 %copy-start.7 = (f32[128]{0:T(128)S(1)}, f32[128]{0:T(128)}, u32[]{:S(2)}) copy-start(f32[128]{0:T(128)} %param.25) | copy-start | bytes 1540
where the time goes:
time: 221 us; the launch traced here: 220 us
  blocking collectives  58.9 us (27%)
  local copies, waits for them, and re-layouts  54.9 us (25%)
  waiting for transfers between devices  38.8 us (18%)
  starting transfers between devices  36.2 us (16%)
  matrix products  23.7 us (11%)
  other arithmetic  6.28 us (3%)
    all_gather x1, blocking collectives, on_device(): gathered = lax.all_gather(flat_normed, 'row', axis=0, tiled=True)  58.9 us
    all_to_all x3, starting transfers between devices, from_everyone(): lax.all_to_all(jnp.broadcast_to(value[None], (count, *value.shape)), axis...  32.5 us
    all_to_all x3, waiting for transfers between devices, from_everyone(): lax.all_to_all(jnp.broadcast_to(value[None], (count, *value.shape)), axis...  27.2 us
    div x3, local copies, waits for them, and re-layouts, outer_block(): jnp.einsum('isc,sjd->ijcd', left_block, right_all, precision=PRECISE)  23.6 us
    another operation x3, local copies, waits for them, and re-layouts  15.1 us
    dot_general x3, matrix products, outer_block(): jnp.einsum('isc,sjd->ijcd', left_block, right_all, precision=PRECISE)  14.8 us
    all_to_all x1, waiting for transfers between devices, on_device(): lax.all_to_all(right_tokens, 'col', split_axis=0, concat_axis=1, tiled=True)  11.7 us
    unnamed x28, local copies, waits for them, and re-layouts  7.25 us
  transfers between devices with their start and end apart: 4, of which 3 were waited for; matrix products, arithmetic and copies ran while one was open for 3% of the time, Pallas kernels for 0%

commit v1 on v0

--- a/solution.py
+++ b/solution.py
@@ -51,7 +51,10 @@
     channels = alignment.shape[2]
     normed = normalize(alignment, align_gain)
     flat_normed = normed.reshape(local_rows, local_seqs * channels)
-    gathered = lax.all_gather(flat_normed, "row", axis=0, tiled=True)
+    size = lax.axis_size("row")
+    blocks = jnp.stack([flat_normed for _ in range(size)])
+    blocks = lax.all_to_all(blocks, "row", split_axis=0, concat_axis=0)
+    gathered = jnp.concatenate(blocks, axis=0)
     gathered = gathered.reshape(-1, local_seqs, channels)
     mixed_rows = jnp.einsum(
         "hij,jsc->ishc", collect(pair_weights, "col", 2), gathered, precision=PRECISE

time: 221 us -> 228 us (1.032)
  blocking collectives: 58.9 us -> 0 us
  waiting for transfers between devices: 38.8 us -> 76.4 us
  starting transfers between devices: 36.2 us -> 61.8 us
  local copies, waits for them, and re-layouts: 54.9 us -> 58 us
    all_gather x1 -> x0, blocking collectives: 58.9 us -> none  [on_device(): gathered = lax.all_gather(flat_normed, 'row', axis=0, tiled=True)]
    all_to_all x0 -> x1, waiting for transfers between devices: none -> 22 us  [on_device(): blocks = lax.all_to_all(blocks, 'row', split_axis=0, concat_axis=0)]
    all_to_all x0 -> x1, starting transfers between devices: none -> 15.7 us  [on_device(): blocks = lax.all_to_all(blocks, 'row', split_axis=0, concat_axis=0)]
    all_to_all x3, waiting for transfers between devices: 27.2 us -> 42.1 us  [from_everyone(): lax.all_to_all(jnp.broadcast_to(value[None], (count, *value.shape)), axis...]
    all_to_all x3, starting transfers between devices: 32.5 us -> 42.6 us  [from_everyone(): lax.all_to_all(jnp.broadcast_to(value[None], (count, *value.shape)), axis...]
    another operation x3 -> x7, local copies, waits for them, and re-layouts: 15.1 us -> 18.7 us
  transfers between devices with their start and end apart: 4 -> 5, of which waited for: 3 -> 5; matrix products, arithmetic and copies ran while one was open for 3% -> 4% of each run, Pallas kernels for 0% -> 0%
where the time goes in v1:
time: 228 us; the launch traced here: 227 us
  waiting for transfers between devices  76.4 us (34%)
  starting transfers between devices  61.8 us (27%)
  local copies, waits for them, and re-layouts  58 us (25%)
  matrix products  23.8 us (10%)
  other arithmetic  6.25 us (3%)
    all_to_all x3, starting transfers between devices, from_everyone(): lax.all_to_all(jnp.broadcast_to(value[None], (count, *value.shape)), axis...  42.6 us
    all_to_all x3, waiting for transfers between devices, from_everyone(): lax.all_to_all(jnp.broadcast_to(value[None], (count, *value.shape)), axis...  42.1 us
    div x3, local copies, waits for them, and re-layouts, outer_block(): jnp.einsum('isc,sjd->ijcd', left_block, right_all, precision=PRECISE)  23.6 us
    all_to_all x1, waiting for transfers between devices, on_device(): blocks = lax.all_to_all(blocks, 'row', split_axis=0, concat_axis=0)  22 us
    all_to_all x1, starting transfers between devices, on_device(): blocks = lax.all_to_all(blocks, 'row', split_axis=0, concat_axis=0)  15.7 us
    another operation x3, local copies, waits for them, and re-layouts  15.1 us
    dot_general x3, matrix products, outer_block(): jnp.einsum('isc,sjd->ijcd', left_block, right_all, precision=PRECISE)  14.9 us
    all_to_all x1, waiting for transfers between devices, on_device(): lax.all_to_all(right_tokens, 'col', split_axis=0, concat_axis=1, tiled=True)  12.4 us
  transfers between devices with their start and end apart: 5, of which 5 were waited for; matrix products, arithmetic and copies ran while one was open for 4% of the time, Pallas kernels for 0%

profile of v1, /device:TPU:8, one launch (start us, length us, event | category | flops | bytes accessed | tf_op | source)
XLA Modules:
  0.0 227.3 jit_solution(10370865455233850683)
XLA Ops:
  0.6 1.1 broadcast_in_dim.13
  1.7 2.4 %reshape.73 = f32[16,1,9216]{2,1,0:T(1,128)} reshape(f32[16,8,24,48]{3,2,1,0:T(8,128)S(1)} %broadcast_in_dim.13) | data formatting | bytes 1179648
  4.1 8.5 %all-to-all-start.1 = ((f32[16,1,9216]{2,1,0:T(1,128)}), f32[16,1,9216]{2,1,0:T(1,128)S(1)}, u32[]{:S(2)}, u32[]{:S(2)}) async-start(f32[16,1,9216]{2,1,0:T(1,128)} %reshape.73), calls=%async_computation.1 | async-start | bytes 1179648 | tf_op jit(solution)/shard_map/all_to_all | solution.py:11
  13.2 16.0 %all-to-all-done.1 = f32[16,1,9216]{2,1,0:T(1,128)S(1)} async-done(((f32[16,1,9216]{2,1,0:T(1,128)}), f32[16,1,9216]{2,1,0:T(1,128)S(1)}, u32[]{:S(2)}, u32[]{:S(2)}) %all-to-all-start.1) | async-done | bytes 589856 | tf_op jit(solution)/shard_map/all_to_all | solution.py:11
  30.1 15.7 %all-to-all-start = ((f32[32,24,256]{2,1,0:T(8,128)}), f32[32,24,256]{2,1,0:T(8,128)}, u32[]{:S(2)}, u32[]{:S(2)}) async-start(f32[32,24,256]{2,1,0:T(8,128)} %stack.3), calls=%async_computation | async-start | bytes 1572864 | tf_op jit(solution)/shard_map/all_to_all | solution.py:56
  46.5 2.0 reduce
  50.1 1.5 reshape.67
  51.6 22.0 %all-to-all-done = f32[32,24,256]{2,1,0:T(8,128)} async-done(((f32[32,24,256]{2,1,0:T(8,128)}), f32[32,24,256]{2,1,0:T(8,128)}, u32[]{:S(2)}, u32[]{:S(2)}) %all-to-all-start) | async-done | bytes 786464 | tf_op jit(solution)/shard_map/all_to_all | solution.py:56
  73.5 1.9 reshape_reshape.6
  76.5 1.1 convolution_bitcast_fusion.2
  80.5 19.3 %all-to-all-start.3 = ((f32[32,24,128]{2,1,0:T(8,128)}), f32[32,24,128]{2,1,0:T(8,128)S(1)}, u32[]{:S(2)}, u32[]{:S(2)}) async-start(f32[32,24,128]{2,1,0:T(8,128)} %broadcast_in_dim.19), calls=%async_computation.3 | async-start | bytes 786432 | tf_op jit(solution)/shard_map/all_to_all | solution.py:11
  100.1 17.5 %all-to-all-done.3 = f32[32,24,128]{2,1,0:T(8,128)S(1)} async-done(((f32[32,24,128]{2,1,0:T(8,128)}), f32[32,24,128]{2,1,0:T(8,128)S(1)}, u32[]{:S(2)}, u32[]{:S(2)}) %all-to-all-start.3) | async-done | bytes 393248 | tf_op jit(solution)/shard_map/all_to_all | solution.py:11
  118.4 14.8 %all-to-all-start.2 = ((f32[16,4,768]{2,1,0:T(4,128)}), f32[16,4,768]{2,1,0:T(4,128)S(1)}, u32[]{:S(2)}, u32[]{:S(2)}) async-start(f32[16,4,768]{2,1,0:T(4,128)} %broadcast_in_dim.16), calls=%async_computation.2 | async-start | bytes 393216 | tf_op jit(solution)/shard_map/all_to_all | solution.py:11
  133.9 1.8 reshape.75
  135.7 8.5 %all-to-all-done.2 = f32[16,4,768]{2,1,0:T(4,128)S(1)} async-done(((f32[16,4,768]{2,1,0:T(4,128)}), f32[16,4,768]{2,1,0:T(4,128)S(1)}, u32[]{:S(2)}, u32[]{:S(2)}) %all-to-all-start.2) | async-done | bytes 196640 | tf_op jit(solution)/shard_map/all_to_all | solution.py:11
  144.1 3.6 %all-to-all-start.4 = ((f32[16,1,6144]{2,1,0:T(1,128)}), f32[16,1,6144]{2,1,0:T(1,128)S(1)}, u32[]{:S(2)}, u32[]{:S(2)}) async-start(f32[16,1,6144]{2,1,0:T(1,128)} %reshape.75), calls=%async_computation.4 | async-start | bytes 786432 | tf_op jit(solution)/shard_map/all_to_all | solution.py:78
  148.9 12.4 %all-to-all-done.4 = f32[16,1,6144]{2,1,0:T(1,128)S(1)} async-done(((f32[16,1,6144]{2,1,0:T(1,128)}), f32[16,1,6144]{2,1,0:T(1,128)S(1)}, u32[]{:S(2)}, u32[]{:S(2)}) %all-to-all-start.4) | async-done | bytes 393248 | tf_op jit(solution)/shard_map/all_to_all | solution.py:78
  161.2 1.5 reduce.1
  165.3 59.8 %while.10 = (s32[]{:T(128)}, f32[3,8,48,128]{3,2,1,0:T(8,128)}, f32[3,8,64,32]{2,3,1,0:T(8,128)S(1)}, f32[64,48,32]{0,1,2:T(8,128)S(1)}, f32[1024,128]{1,0:T(8,128)S(1)}, /*index=5*/s32[]{:T(128)}) while((s32[]{:T(128)}, f32[3,8,48,128]{3,2,1,0:T(8,128)}, f32[3,8,64,32]{2,3,1,0:T(8,128)S(1)}, f32[64,48,32]{0,1,2:T(8,128)S(1)}, ...), condition=%wide.region_5.6_spmd, body=%wide.region_4.5_spmd.sunk | while | flops 906362880 | bytes 11076169 | solution.py:96
  165.3 5.0 %multiply_bitcast_fusion.2 = f32[8,48,32,32]{1,2,3,0:T(8,128)} fusion(f32[64,48,32]{0,1,2:T(8,128)S(1)} %get-tuple-element.118, f32[3,8,64,32]{2,3,1,0:T(8,128)S(1)} %get-tuple-element.117, s32[]{:T(128)} %get-tuple-element.109), kind=kOutput, calls=%fused_computation.clone.1 | convolution fusion | flops 302383104 | bytes 2490372 | tf_op jit(solution)/shard_map/while/body/eval_jaxpr/isc,sjd->ijcd/dot_general | solution.py:89
  170.3 7.9 %copy.92 = f32[8,48,32,32]{3,2,1,0:T(8,128)} copy(f32[8,48,32,32]{1,2,3,0:T(8,128)} %multiply_bitcast_fusion.2) | data formatting | bytes 3145728 | tf_op jit(solution)/shard_map/while/body/eval_jaxpr/div | solution.py:89
  178.2 5.0 %reshape.78 = f32[8,48,1024]{2,1,0:T(8,128)S(1)} reshape(f32[8,48,32,32]{3,2,1,0:T(8,128)} %copy.92) | data formatting | bytes 3145728 | tf_op jit(solution)/shard_map/reshape.24
  183.2 2.1 fusion.39
  185.3 5.0 %multiply_bitcast_fusion.2 = f32[8,48,32,32]{1,2,3,0:T(8,128)} fusion(f32[64,48,32]{0,1,2:T(8,128)S(1)} %get-tuple-element.118, f32[3,8,64,32]{2,3,1,0:T(8,128)S(1)} %get-tuple-element.117, s32[]{:T(128)} %get-tuple-element.109), kind=kOutput, calls=%fused_computation.clone.1 | convolution fusion | flops 302383104 | bytes 2490372 | tf_op jit(solution)/shard_map/while/body/eval_jaxpr/isc,sjd->ijcd/dot_general | solution.py:89
  190.2 7.9 %copy.92 = f32[8,48,32,32]{3,2,1,0:T(8,128)} copy(f32[8,48,32,32]{1,2,3,0:T(8,128)} %multiply_bitcast_fusion.2) | data formatting | bytes 3145728 | tf_op jit(solution)/shard_map/while/body/eval_jaxpr/div | solution.py:89
  198.1 5.0 %reshape.78 = f32[8,48,1024]{2,1,0:T(8,128)S(1)} reshape(f32[8,48,32,32]{3,2,1,0:T(8,128)} %copy.92) | data formatting | bytes 3145728 | tf_op jit(solution)/shard_map/reshape.24
  203.1 2.1 fusion.39
  205.2 5.0 %multiply_bitcast_fusion.2 = f32[8,48,32,32]{1,2,3,0:T(8,128)} fusion(f32[64,48,32]{0,1,2:T(8,128)S(1)} %get-tuple-element.118, f32[3,8,64,32]{2,3,1,0:T(8,128)S(1)} %get-tuple-element.117, s32[]{:T(128)} %get-tuple-element.109), kind=kOutput, calls=%fused_computation.clone.1 | convolution fusion | flops 302383104 | bytes 2490372 | tf_op jit(solution)/shard_map/while/body/eval_jaxpr/isc,sjd->ijcd/dot_general | solution.py:89
  210.2 7.9 %copy.92 = f32[8,48,32,32]{3,2,1,0:T(8,128)} copy(f32[8,48,32,32]{1,2,3,0:T(8,128)} %multiply_bitcast_fusion.2) | data formatting | bytes 3145728 | tf_op jit(solution)/shard_map/while/body/eval_jaxpr/div | solution.py:89
  218.1 5.0 %reshape.78 = f32[8,48,1024]{2,1,0:T(8,128)S(1)} reshape(f32[8,48,32,32]{3,2,1,0:T(8,128)} %copy.92) | data formatting | bytes 3145728 | tf_op jit(solution)/shard_map/reshape.24
  223.1 2.1 fusion.39
  225.2 2.1 fusion.11
  (57 shorter events, 12.9 us)
Async XLA Ops:
  0.6 77.9 %copy-start = (f32[64,256]{1,0:T(8,128)S(1)}, f32[64,256]{1,0:T(8,128)}, u32[]{:S(2)}) copy-start(f32[64,256]{1,0:T(8,128)} %param.19) | copy-start | bytes 196612
  1.7 10.9 %copy-start.3 = (f32[24,4,64]{2,1,0:T(4,128)S(1)}, f32[24,4,64]{2,1,0:T(4,128)}, u32[]{:S(2)}) copy-start(f32[24,4,64]{2,1,0:T(4,128)} %param.14) | copy-start | bytes 73732
  1.7 11.2 %copy-start.6 = (f32[64]{0:T(128)S(1)}, f32[64]{0:T(128)}, u32[]{:S(2)}) copy-start(f32[64]{0:T(128)} %param.17) | copy-start | bytes 772
  4.1 25.1 %all-to-all-start.1 = ((f32[16,1,9216]{2,1,0:T(1,128)}), f32[16,1,9216]{2,1,0:T(1,128)S(1)}, u32[]{:S(2)}, u32[]{:S(2)}) async-start(f32[16,1,9216]{2,1,0:T(1,128)} %reshape.73), calls=%async_computation.1 | async-start | bytes 1179648 | tf_op jit(solution)/shard_map/all_to_all | solution.py:11
  12.6 33.2 %copy-start.4 = (f32[64,256]{1,0:T(8,128)S(1)}, f32[64,256]{1,0:T(8,128)}, u32[]{:S(2)}) copy-start(f32[64,256]{1,0:T(8,128)} %param.18) | copy-start | bytes 196612
  30.1 43.4 %all-to-all-start = ((f32[32,24,256]{2,1,0:T(8,128)}), f32[32,24,256]{2,1,0:T(8,128)}, u32[]{:S(2)}, u32[]{:S(2)}) async-start(f32[32,24,256]{2,1,0:T(8,128)} %stack.3), calls=%async_computation | async-start | bytes 1572864 | tf_op jit(solution)/shard_map/all_to_all | solution.py:56
  75.4 1.1 copy-start.2
  77.6 1.2 copy-start.5
  77.6 1.7 copy-start.8
  77.6 1.7 copy-start.10
  78.1 21.6 %copy-start.9 = (f32[64,32]{0,1:T(8,128)S(1)}, f32[64,32]{0,1:T(8,128)}, u32[]{:S(2)}) copy-start(f32[64,32]{0,1:T(8,128)} %param.22) | copy-start | bytes 24580
  80.5 37.2 %all-to-all-start.3 = ((f32[32,24,128]{2,1,0:T(8,128)}), f32[32,24,128]{2,1,0:T(8,128)S(1)}, u32[]{:S(2)}, u32[]{:S(2)}) async-start(f32[32,24,128]{2,1,0:T(8,128)} %broadcast_in_dim.19), calls=%async_computation.3 | async-start | bytes 786432 | tf_op jit(solution)/shard_map/all_to_all | solution.py:11
  118.4 25.8 %all-to-all-start.2 = ((f32[16,4,768]{2,1,0:T(4,128)}), f32[16,4,768]{2,1,0:T(4,128)S(1)}, u32[]{:S(2)}, u32[]{:S(2)}) async-start(f32[16,4,768]{2,1,0:T(4,128)} %broadcast_in_dim.16), calls=%async_computation.2 | async-start | bytes 393216 | tf_op jit(solution)/shard_map/all_to_all | solution.py:11
  144.1 17.1 %all-to-all-start.4 = ((f32[16,1,6144]{2,1,0:T(1,128)}), f32[16,1,6144]{2,1,0:T(1,128)S(1)}, u32[]{:S(2)}, u32[]{:S(2)}) async-start(f32[16,1,6144]{2,1,0:T(1,128)} %reshape.75), calls=%async_computation.4 | async-start | bytes 786432 | tf_op jit(solution)/shard_map/all_to_all | solution.py:78
  164.3 1.0 copy-start.1
  165.3 59.8 %copy-start.7 = (f32[128]{0:T(128)S(1)}, f32[128]{0:T(128)}, u32[]{:S(2)}) copy-start(f32[128]{0:T(128)} %param.25) | copy-start | bytes 1540
